TPU v7x, 32 devices: a whole 2x2x4 slice. The times are simulated.
32 devices in a mesh: blk: 8 (over z, y), tp: 4 (over x, core).
Axes of the slice: x: 2, y: 2, z: 4, core: 2. Of those that a mesh axis runs over, the one named last changes fastest.
Arguments:
- tokens: bfloat16 [3072, 4096], P('blk'), may hold values from -48 to 48
- w_query: bfloat16 [4096, 2048], P('blk', 'tp'), may hold values from -0.09375 to 0.09375
- key_weight: bfloat16 [4096, 512], P('blk', 'tp'), may hold values from -0.09375 to 0.09375
- value_weight: bfloat16 [4096, 512], P('blk', 'tp'), may hold values from -0.09375 to 0.09375
- w_output: bfloat16 [2048, 4096], P('tp', 'blk'), may hold values from -0.125 to 0.125
- out_grad: bfloat16 [3072, 4096], P('blk'), may hold values from -3 to 3
Outputs:
- attn_out: bfloat16 [3072, 4096], P('blk', 'tp')
- tokens_grad: bfloat16 [3072, 4096], P('blk', 'tp')
- query_grad: float32 [4096, 2048], P('blk', 'tp')
- key_grad: float32 [4096, 512], P('blk', 'tp')
- value_grad: float32 [4096, 512], P('blk', 'tp')
- output_grad: float32 [2048, 4096], P('tp', 'blk')
All inputs are finite; a program needn't handle non-finite values.
Results may differ from a plain program's by a relative error of at most 0.005.
The roundings to bfloat16 on the way count: a program that leaves them out, or rounds other values in their place, can miss the bound.
Values may be sent and summed in bfloat16 or wider, within the bound.
A program may use at most 128 MiB of HBM per device.

v0:
```python
import math

import jax
import jax.numpy as jnp
from jax import lax
from jax.sharding import PartitionSpec as P

HEAD_SIZE = 128


def transposed_product(first_operand, second_operand):
    return lax.dot_general(
        first_operand, second_operand, (((1,), (1,)), ((), ())), preferred_element_type=jnp.float32
    )


def leading_product(first_operand, second_operand):
    return lax.dot_general(
        first_operand, second_operand, (((0,), (0,)), ((), ())), preferred_element_type=jnp.float32
    )


def causal_probs(query_block, key_head_rows, first_row, score_scale):
    scores = (
        jnp.einsum("tkgd,skd->kgts", query_block, key_head_rows, preferred_element_type=jnp.float32)
        * score_scale
    )
    row_index = first_row + lax.broadcasted_iota(jnp.int32, scores.shape, 2)
    col_index = lax.broadcasted_iota(jnp.int32, scores.shape, 3)
    scores = jnp.where(col_index <= row_index, scores, -jnp.inf)
    row_max = jnp.max(scores, axis=-1, keepdims=True)
    powered = jnp.exp(scores - row_max)
    return powered / jnp.sum(powered, axis=-1, keepdims=True)


def on_device(tokens, w_query, key_weight, value_weight, w_output, out_grad):
    sequence_length = tokens.shape[0]
    head_cols = w_query.shape[1]
    kv_cols = key_weight.shape[1]
    local_kv = kv_cols // HEAD_SIZE
    group_width = head_cols // kv_cols
    block_count = sequence_length // sequence_length
    score_scale = 1.0 / math.sqrt(HEAD_SIZE)
    output_rows = lax.all_gather(w_output, "blk", axis=1, tiled=True)
    query_rows, key_rows, value_rows = (
        lax.all_gather(w_query, "blk", axis=0, tiled=True),
        lax.all_gather(key_weight, "blk", axis=0, tiled=True),
        lax.all_gather(value_weight, "blk", axis=0, tiled=True),
    )
    query_full = jnp.dot(tokens, query_rows, preferred_element_type=jnp.float32)
    key_full = jnp.dot(tokens, key_rows, preferred_element_type=jnp.float32)
    value_full = jnp.dot(tokens, value_rows, preferred_element_type=jnp.float32)
    query_activation = query_full.astype(jnp.bfloat16)
    query_head_rows = query_activation.reshape(sequence_length, local_kv, group_width, HEAD_SIZE)
    key_activation = key_full.astype(jnp.bfloat16)
    key_head_rows = key_activation.reshape(sequence_length, local_kv, HEAD_SIZE)
    value_head_rows = value_full.astype(jnp.bfloat16).reshape(sequence_length, local_kv, HEAD_SIZE)
    block_ids = jnp.arange(block_count, dtype=jnp.int32)

    def forward_block(ignored, block_index):
        first_row = block_index * sequence_length
        soft_weights = causal_probs(query_head_rows, key_head_rows, first_row, score_scale).astype(
            jnp.bfloat16
        )
        head_block = jnp.einsum(
            "kgts,skd->tkgd", soft_weights, value_head_rows, preferred_element_type=jnp.float32
        )
        return (ignored, head_block.astype(jnp.bfloat16))

    ignored_carry, mix_blocks = lax.scan(forward_block, jnp.zeros((), jnp.int32), block_ids)
    head_mix = mix_blocks.reshape(sequence_length, head_cols)
    out_term = jnp.dot(head_mix, output_rows, preferred_element_type=jnp.float32)
    attn_out = lax.psum_scatter(out_term, "tp", scatter_dimension=1, tiled=True).astype(
        jnp.bfloat16
    )
    heads_gradient = (
        transposed_product(out_grad, output_rows)
        .astype(jnp.bfloat16)
        .reshape(sequence_length, local_kv, group_width, HEAD_SIZE)
    )

    def backward_block(kv_sums, block_index):
        first_row = block_index * sequence_length
        probs = causal_probs(query_head_rows, key_head_rows, first_row, score_scale)
        soft_weights = probs.astype(jnp.bfloat16)
        grad_probs = jnp.einsum(
            "tkgd,skd->kgts", heads_gradient, value_head_rows, preferred_element_type=jnp.float32
        )
        row_delta = jnp.sum(probs * grad_probs, axis=-1, keepdims=True)
        scores_gradient = (probs * (grad_probs - row_delta) * score_scale).astype(jnp.bfloat16)
        grad_query = jnp.einsum(
            "kgts,skd->tkgd", scores_gradient, key_head_rows, preferred_element_type=jnp.float32
        )
        key_total = kv_sums[0] + jnp.einsum(
            "uxyi,yuxz->iuz", scores_gradient, query_head_rows, preferred_element_type=jnp.float32
        )
        value_total = kv_sums[1] + jnp.einsum(
            "uxyi,yuxz->iuz", soft_weights, heads_gradient, preferred_element_type=jnp.float32
        )
        return ((key_total, value_total), grad_query.astype(jnp.bfloat16))

    empty_kv = jnp.zeros((sequence_length, local_kv, HEAD_SIZE), jnp.float32)
    kv_totals, query_blocks = lax.scan(backward_block, (empty_kv, empty_kv), block_ids)
    grad_query = query_blocks.reshape(sequence_length, head_cols)
    key_gradient = kv_totals[0].astype(jnp.bfloat16).reshape(sequence_length, kv_cols)
    value_gradient = kv_totals[1].astype(jnp.bfloat16).reshape(sequence_length, kv_cols)
    input_term = (
        transposed_product(grad_query, query_rows)
        + transposed_product(key_gradient, key_rows)
        + transposed_product(value_gradient, value_rows)
    )
    tokens_grad = lax.psum_scatter(input_term, "tp", scatter_dimension=1, tiled=True).astype(
        jnp.bfloat16
    )
    joined_grads = jnp.concatenate([grad_query, key_gradient, value_gradient], axis=1)
    joint_grad = lax.psum_scatter(
        leading_product(tokens, joined_grads), "blk", scatter_dimension=0, tiled=True
    )
    query_grad = joint_grad[:, :head_cols]
    key_grad = joint_grad[:, head_cols : head_cols + kv_cols]
    value_grad = joint_grad[:, head_cols + kv_cols :]
    output_term = leading_product(head_mix, out_grad)
    output_grad = lax.psum_scatter(output_term, "blk", scatter_dimension=1, tiled=True)
    return (attn_out, tokens_grad, query_grad, key_grad, value_grad, output_grad)


def solution(mesh):
    placed = (
        P("blk", None),
        P("blk", "tp"),
        P("blk", "tp"),
        P("blk", "tp"),
        P("tp", "blk"),
        P("blk", None),
    )
    return jax.shard_map(
        on_device,
        mesh=mesh,
        in_specs=placed,
        out_specs=(
            P("blk", "tp"),
            P("blk", "tp"),
            P("blk", "tp"),
            P("blk", "tp"),
            P("blk", "tp"),
            P("tp", "blk"),
        ),
        check_vma=False,
    )
```

profile of v0, /device:TPU:0, one launch (start us, length us, event | category | flops | bytes accessed | tf_op | source)
XLA Modules:
  0.0 738.9 jit_solution(15159800904259940518)
XLA Ops:
  10.0 43.0 %all-gather.5.cloned.1.call-done = bf16[4096,128]{1,0:T(8,128)(2,1)} async-done(((bf16[512,128]{1,0:T(8,128)(2,1)}), bf16[4096,128]{1,0:T(8,128)(2,1)}) %all-gather.5.cloned.1.call-update) | async-done | bytes 1048592 | tf_op jit(solution)/shard_map/all_gather | solution.py:48
  53.0 2.8 fusion.21
  55.9 38.2 %all-gather.7.cloned.1.call-done = bf16[4096,128]{1,0:T(8,128)(2,1)} async-done(((bf16[512,128]{1,0:T(8,128)(2,1)}), bf16[4096,128]{1,0:T(8,128)(2,1)}) %all-gather.7.cloned.1.call-update) | async-done | bytes 1048592 | tf_op jit(solution)/shard_map/all_gather | solution.py:47
  94.1 2.8 fusion.22
  96.9 71.5 %all-gather.9.cloned.1.call-done = bf16[4096,512]{1,0:T(8,128)(2,1)} async-done(((bf16[512,512]{1,0:T(8,128)(2,1)}), bf16[4096,512]{1,0:T(8,128)(2,1)}) %all-gather.9.cloned.1.call-update) | async-done | bytes 4194320 | tf_op jit(solution)/shard_map/all_gather | solution.py:46
  168.4 4.7 convolution_convert_fusion.3
  173.1 1.2 copy.33
  174.4 1.5 fusion.34
  176.3 1.1 copy-done.1
  178.0 65.6 %all-gather.11.cloned.1.call-done = bf16[512,4096]{1,0:T(8,128)(2,1)} async-done(((bf16[512,512]{1,0:T(8,128)(2,1)}), bf16[512,4096]{1,0:T(8,128)(2,1)}) %all-gather.11.cloned.1.call-update) | async-done | bytes 4194320 | tf_op jit(solution)/shard_map/all_gather | solution.py:44
  243.6 6.7 fusion.35
  250.6 5.7 convolution_convert_fusion.2
  256.3 1.4 copy.34
  257.7 3.1 fusion
  263.3 1.0 fusion.37
  264.9 1.6 copy-done.5
  266.6 1.9 fusion.36
  268.5 3.7 add_add_fusion
  272.2 7.3 convolution_bitcast_fusion
  279.6 0.9 copy-done.7
  280.5 7.5 %fusion.38 = f32[512,4096]{1,0:T(8,128)} fusion(bf16[384,512]{0,1:T(8,128)(2,1)S(1)} %bitcast.108, bf16[384,4096]{1,0:T(8,128)(2,1)} %param.11), kind=kOutput, calls=%fused_computation.44 | convolution fusion | flops 1610612736 | bytes 11927552 | tf_op jit(solution)/shard_map/dot_general | solution.py:18
  288.1 19.0 %reduce-scatter.5.cloned.1.call-done = f32[384,1024]{1,0:T(8,128)} async-done(((f32[384,4096]{1,0:T(8,128)}), f32[384,1024]{1,0:T(8,128)}) %reduce-scatter.5.cloned.1.call-update) | async-done | bytes 1572880 | tf_op jit(solution)/shard_map/reduce_scatter | solution.py:73
  307.1 2.4 convert_element_type.73
  309.5 58.5 %reduce-scatter.7.cloned.1.call-done = f32[384,1024]{1,0:T(8,128)} async-done(((f32[384,4096]{1,0:T(8,128)}), f32[384,1024]{1,0:T(8,128)}) %reduce-scatter.7.cloned.1.call-update) | async-done | bytes 1572880 | tf_op jit(solution)/shard_map/reduce_scatter | solution.py:112
  368.0 2.4 convert_element_type.85
  370.4 208.9 %reduce-scatter.9.cloned.1.call-done = f32[512,768]{0,1:T(8,128)} async-done(((f32[4096,768]{0,1:T(8,128)}), f32[512,768]{0,1:T(8,128)}) %reduce-scatter.9.cloned.1.call-update) | async-done | bytes 1572880 | tf_op jit(solution)/shard_map/reduce_scatter | solution.py:116
  579.3 2.3 slice.12
  581.6 2.5 copy.22
  584.1 1.8 fusion.33
  585.9 1.8 copy.24
  587.6 0.8 copy.23
  588.5 143.5 %reduce-scatter.11.cloned.1.call-done = f32[512,512]{1,0:T(8,128)} async-done(((f32[512,4096]{1,0:T(8,128)}), f32[512,512]{1,0:T(8,128)}) %reduce-scatter.11.cloned.1.call-update) | async-done | bytes 1048592 | tf_op jit(solution)/shard_map/reduce_scatter | solution.py:123
  (51 shorter events, 7.1 us)
Async XLA Ops:
  7.2 45.9 %copy-start = (bf16[384,4096]{1,0:T(8,128)(2,1)S(1)}, bf16[384,4096]{1,0:T(8,128)(2,1)}, u32[]{:S(2)}) copy-start(bf16[384,4096]{1,0:T(8,128)(2,1)} %param.6) | copy-start | bytes 9437188
  7.2 45.8 %all-gather.5.cloned.1.call-start = ((), (), s32[]{:S(2)}) async-start(), calls=%async_computation.4 | async-start | bytes 1179648 | tf_op jit(solution)/shard_map/all_gather | solution.py:48
  7.9 86.2 %all-gather.7.cloned.1.call-start = ((), (), s32[]{:S(2)}) async-start(), calls=%async_computation.5 | async-start | bytes 1179648 | tf_op jit(solution)/shard_map/all_gather | solution.py:47
  8.7 159.7 %all-gather.9.cloned.1.call-start = ((), (), s32[]{:S(2)}) async-start(), calls=%async_computation.6 | async-start | bytes 4718592 | tf_op jit(solution)/shard_map/all_gather | solution.py:46
  9.4 234.2 %all-gather.11.cloned.1.call-start = ((), (), s32[]{:S(2)}) async-start(), calls=%async_computation.7 | async-start | bytes 4718592 | tf_op jit(solution)/shard_map/all_gather | solution.py:44
  10.0 297.1 %reduce-scatter.5.cloned.1.call-start = ((), (), s32[]{:S(2)}) async-start(), calls=%async_computation.8 | async-start | bytes 7864320 | tf_op jit(solution)/shard_map/reduce_scatter | solution.py:73
  174.3 1.6 copy-start.8
  174.3 3.1 copy-start.15
  175.9 1.5 copy-start.1
  178.0 72.3 %copy-start.6 = (bf16[128,4,384]{2,0,1:T(8,128)(2,1)}, bf16[128,4,384]{2,0,1:T(8,128)(2,1)S(1)}, u32[]{:S(2)}) copy-start(bf16[128,4,384]{2,0,1:T(8,128)(2,1)S(1)} %convolution_convert_fusion.1) | copy-start | bytes 1179652
  250.3 117.7 %reduce-scatter.7.cloned.1.call-start = ((), (), s32[]{:S(2)}) async-start(), calls=%async_computation.9 | async-start | bytes 7864320 | tf_op jit(solution)/shard_map/reduce_scatter | solution.py:112
  257.6 3.2 copy-start.12
  257.6 3.4 copy-start.2
  261.0 1.0 copy-start.9
  261.0 1.5 copy-start.14
  262.0 1.3 copy-start.4
  262.6 1.8 copy-start.10
  263.3 1.0 copy-start.13
  264.3 2.2 copy-start.5
  264.9 3.5 copy-start.11
  266.6 1.9 copy-start.3
  272.2 307.1 %reduce-scatter.9.cloned.1.call-start = ((), (), s32[]{:S(2)}) async-start(), calls=%async_computation.10 | async-start | bytes 14155776 | tf_op jit(solution)/shard_map/reduce_scatter | solution.py:116
  279.5 1.0 copy-start.7
  279.5 452.5 %reduce-scatter.11.cloned.1.call-start = ((), (), s32[]{:S(2)}) async-start(), calls=%async_computation.11 | async-start | bytes 9437184 | tf_op jit(solution)/shard_map/reduce_scatter | solution.py:123
Sparse Core Ops, SparseCore 0:
  10.1 42.8 all-gather.4
  55.1 38.8 all-gather.6
  96.2 72.1 all-gather.8
  170.3 73.2 all-gather.10
  250.5 56.5 reduce-scatter.4
  309.6 58.3 reduce-scatter.6
  371.6 207.6 reduce-scatter.8
  583.5 148.5 reduce-scatter.10
where the time goes:
time: 740 us; the launch traced here: 739 us
  waiting for transfers between devices  651 us (88%)
  matrix products  50.9 us (7%)
  local copies, waits for them, and re-layouts  16.4 us (2%)
  between operations  14.3 us (2%)
    reduce_scatter x1, waiting for transfers between devices, on_device(): lax.psum_scatter(leading_product(tokens, joined_grads), 'blk', scatter_di...  209 us
    reduce_scatter x1, waiting for transfers between devices, on_device(): lax.psum_scatter(output_term, 'blk', scatter_dimension=1, tiled=True)  144 us
    all_gather x1, waiting for transfers between devices, on_device(): lax.all_gather(w_query, 'blk', axis=0, tiled=True)  71.5 us
    all_gather x1, waiting for transfers between devices, on_device(): output_rows = lax.all_gather(w_output, 'blk', axis=1, tiled=True)  65.6 us
    reduce_scatter x1, waiting for transfers between devices, on_device(): lax.psum_scatter(input_term, 'tp', scatter_dimension=1, tiled=True)  58.5 us
    all_gather x1, waiting for transfers between devices, on_device(): lax.all_gather(value_weight, 'blk', axis=0, tiled=True)  43 us
    all_gather x1, waiting for transfers between devices, on_device(): lax.all_gather(key_weight, 'blk', axis=0, tiled=True)  38.2 us
    reduce_scatter x1, waiting for transfers between devices, on_device(): lax.psum_scatter(out_term, 'tp', scatter_dimension=1, tiled=True)  19 us
  transfers between devices with their start and end apart: 8, of which 8 were waited for; matrix products, arithmetic and copies ran while one was open for 8% of the time, Pallas kernels for 0%

commit v1 on v0

--- a/solution.py
+++ b/solution.py
@@ -33,6 +33,24 @@
     return powered / jnp.sum(powered, axis=-1, keepdims=True)
 
 
+def column_blocks(tokens, out_grad, tp_count, blk_count):
+    rows, width = tokens.shape
+    part = rows // tp_count
+    cols = width // blk_count
+    first = lax.axis_index("tp") * part
+    sent = jnp.stack(
+        [
+            lax.dynamic_slice_in_dim(tokens, first, part, 0),
+            lax.dynamic_slice_in_dim(out_grad, first, part, 0),
+        ]
+    )
+    sent = sent.reshape(2, part, blk_count, cols).transpose(2, 0, 1, 3)
+    landed = lax.all_to_all(sent, "blk", 0, 0, tiled=True)
+    whole = lax.all_gather(landed, "tp", axis=0)
+    whole = jnp.transpose(whole, (2, 1, 0, 3, 4)).reshape(2, blk_count * rows, cols)
+    return (whole[0], whole[1])
+
+
 def on_device(tokens, w_query, key_weight, value_weight, w_output, out_grad):
     sequence_length = tokens.shape[0]
     head_cols = w_query.shape[1]
@@ -41,12 +59,15 @@
     group_width = head_cols // kv_cols
     block_count = sequence_length // sequence_length
     score_scale = 1.0 / math.sqrt(HEAD_SIZE)
-    output_rows = lax.all_gather(w_output, "blk", axis=1, tiled=True)
-    query_rows, key_rows, value_rows = (
-        lax.all_gather(w_query, "blk", axis=0, tiled=True),
-        lax.all_gather(key_weight, "blk", axis=0, tiled=True),
-        lax.all_gather(value_weight, "blk", axis=0, tiled=True),
-    )
+    tp_count = lax.axis_size("tp")
+    blk_count = lax.axis_size("blk")
+    weight_block = jnp.concatenate([w_query, key_weight, value_weight, w_output.T], axis=1)
+    weight_rows = lax.all_gather(weight_block, "blk", axis=0, tiled=True)
+    query_rows = weight_rows[:, :head_cols]
+    key_rows = weight_rows[:, head_cols : head_cols + kv_cols]
+    value_rows = weight_rows[:, head_cols + kv_cols : head_cols + 2 * kv_cols]
+    output_cols = weight_rows[:, head_cols + 2 * kv_cols :]
+    inputs_by_cols = column_blocks(tokens, out_grad, tp_count, blk_count)
     query_full = jnp.dot(tokens, query_rows, preferred_element_type=jnp.float32)
     key_full = jnp.dot(tokens, key_rows, preferred_element_type=jnp.float32)
     value_full = jnp.dot(tokens, value_rows, preferred_element_type=jnp.float32)
@@ -69,12 +90,12 @@
 
     ignored_carry, mix_blocks = lax.scan(forward_block, jnp.zeros((), jnp.int32), block_ids)
     head_mix = mix_blocks.reshape(sequence_length, head_cols)
-    out_term = jnp.dot(head_mix, output_rows, preferred_element_type=jnp.float32)
+    out_term = transposed_product(head_mix, output_cols)
     attn_out = lax.psum_scatter(out_term, "tp", scatter_dimension=1, tiled=True).astype(
         jnp.bfloat16
     )
     heads_gradient = (
-        transposed_product(out_grad, output_rows)
+        jnp.dot(out_grad, output_cols, preferred_element_type=jnp.float32)
         .astype(jnp.bfloat16)
         .reshape(sequence_length, local_kv, group_width, HEAD_SIZE)
     )
@@ -112,15 +133,15 @@
     tokens_grad = lax.psum_scatter(input_term, "tp", scatter_dimension=1, tiled=True).astype(
         jnp.bfloat16
     )
+    mix_all = lax.all_gather(head_mix, "blk", axis=0, tiled=True)
     joined_grads = jnp.concatenate([grad_query, key_gradient, value_gradient], axis=1)
-    joint_grad = lax.psum_scatter(
-        leading_product(tokens, joined_grads), "blk", scatter_dimension=0, tiled=True
-    )
+    grads_all = lax.all_gather(joined_grads, "blk", axis=0, tiled=True)
+    tokens_cols, out_grad_cols = inputs_by_cols
+    joint_grad = leading_product(tokens_cols, grads_all)
     query_grad = joint_grad[:, :head_cols]
     key_grad = joint_grad[:, head_cols : head_cols + kv_cols]
     value_grad = joint_grad[:, head_cols + kv_cols :]
-    output_term = leading_product(head_mix, out_grad)
-    output_grad = lax.psum_scatter(output_term, "blk", scatter_dimension=1, tiled=True)
+    output_grad = leading_product(mix_all, out_grad_cols)
     return (attn_out, tokens_grad, query_grad, key_grad, value_grad, output_grad)
 
 

time: 740 us -> 522 us (0.71)
  waiting for transfers between devices: 651 us -> 350 us
  blocking collectives: 0 us -> 81.6 us
    reduce_scatter x2 -> x0, waiting for transfers between devices: 352 us -> none  [the longest x1 209 us: on_device(): lax.psum_scatter(leading_product(tokens, joined_grads), 'blk', scatter_di...]
    all_to_all x0 -> x1, blocking collectives: none -> 81.6 us  [column_blocks(): landed = lax.all_to_all(sent, 'blk', 0, 0, tiled=True)]
    reduce_scatter x1, waiting for transfers between devices: 19 us -> 52.1 us  [on_device(): lax.psum_scatter(out_term, 'tp', scatter_dimension=1, tiled=True)]
    all_gather x4, waiting for transfers between devices: 218 us -> 240 us  [the longest x1 100 us: on_device(): weight_rows = lax.all_gather(weight_block, 'blk', axis=0, tiled=True)]
  transfers between devices with their start and end apart: 8 -> 6, of which waited for: 8 -> 6; matrix products, arithmetic and copies ran while one was open for 8% -> 12% of each run, Pallas kernels for 0% -> 0%
where the time goes in v1:
time: 522 us; the launch traced here: 521 us
  waiting for transfers between devices  350 us (67%)
  blocking collectives  81.6 us (16%)
  matrix products  48.1 us (9%)
  local copies, waits for them, and re-layouts  16.9 us (3%)
  between operations  14.4 us (3%)
  other arithmetic  9.21 us (2%)
    all_gather x1, waiting for transfers between devices, on_device(): weight_rows = lax.all_gather(weight_block, 'blk', axis=0, tiled=True)  100 us
    all_to_all x1, blocking collectives, column_blocks(): landed = lax.all_to_all(sent, 'blk', 0, 0, tiled=True)  81.6 us
    all_gather x1, waiting for transfers between devices, on_device(): grads_all = lax.all_gather(joined_grads, 'blk', axis=0, tiled=True)  76 us
    reduce_scatter x1, waiting for transfers between devices, on_device(): lax.psum_scatter(input_term, 'tp', scatter_dimension=1, tiled=True)  58.5 us
    all_gather x1, waiting for transfers between devices, on_device(): mix_all = lax.all_gather(head_mix, 'blk', axis=0, tiled=True)  58.4 us
    reduce_scatter x1, waiting for transfers between devices, on_device(): lax.psum_scatter(out_term, 'tp', scatter_dimension=1, tiled=True)  52.1 us
    dot_general x4, matrix products, transposed_product(): lax.dot_general(first_operand, second_operand, (((1,), (1,)), ((), ())),...  18 us
    dot_general x2, matrix products, leading_product(): lax.dot_general(first_operand, second_operand, (((0,), (0,)), ((), ())),...  10.7 us
  transfers between devices with their start and end apart: 6, of which 6 were waited for; matrix products, arithmetic and copies ran while one was open for 12% of the time, Pallas kernels for 0%

profile of v1, /device:TPU:0, one launch (start us, length us, event | category | flops | bytes accessed | tf_op | source)
XLA Modules:
  0.0 520.9 jit_solution(2294398787974512257)
XLA Ops:
  7.2 1.2 copy.76
  8.4 1.0 copy.77
  9.4 2.0 copy.75
  11.5 2.4 pad_maximum_fusion
  13.9 1.2 constant_dynamic-slice_fusion
  16.4 81.6 %all_to_all.5 = bf16[8,2,96,512]{3,2,1,0:T(8,128)(2,1)} all-to-all(bf16[8,2,96,512]{3,2,1,0:T(8,128)(2,1)S(1)} %copy.86), channel_id=1, replica_groups=mesh['blk'=8,'tp'=4] {'blk'}, dimensions={0} | all-to-all | bytes 3145728 | tf_op jit(solution)/shard_map/all_to_all | solution.py:48
  98.1 100.0 %all-gather.6.cloned.1.call-done = bf16[4096,1280]{0,1:T(8,128)(2,1)} async-done(((bf16[512,1280]{0,1:T(8,128)(2,1)}), bf16[4096,1280]{0,1:T(8,128)(2,1)}) %all-gather.6.cloned.1.call-update) | async-done | bytes 10485776 | tf_op jit(solution)/shard_map/all_gather | solution.py:65
  198.1 2.3 fusion.36
  200.4 4.6 fusion.14
  205.8 3.0 fusion.35
  208.8 1.3 convolution_convert_fusion.1
  210.3 5.6 %fusion.17 = bf16[512,384]{1,0:T(8,128)(2,1)S(1)} fusion(bf16[384,4096]{1,0:T(8,128)(2,1)} %param.11, bf16[4096,1280]{0,1:T(8,128)(2,1)} %all-gather.6.cloned.1.call-done), kind=kOutput, calls=%fused_computation.25 | convolution fusion | flops 1610809344 | bytes 7733248 | tf_op jit(solution)/shard_map/dot_general | solution.py:98
  216.6 1.0 copy-done.4
  219.7 0.9 pad_maximum_fusion.1
  220.9 6.6 %fusion.2 = f32[384,4096]{1,0:T(8,128)} fusion(bf16[384,512]{0,1:T(8,128)(2,1)S(1)} %bitcast.124, bf16[4096,1280]{0,1:T(8,128)(2,1)} %all-gather.6.cloned.1.call-done), kind=kOutput, calls=%fused_computation.3 | convolution fusion | flops 1610612736 | bytes 10878976 | tf_op jit(solution)/shard_map/dot_general | solution.py:12
  227.6 2.2 fusion.37
  229.8 4.1 fusion.4
  234.0 5.0 add_add_fusion
  238.9 5.3 %all-gather.12.cloned.1.call-done = bf16[32,2,96,512]{3,2,1,0:T(8,128)(2,1)} async-done(((bf16[8,2,96,512]{3,2,1,0:T(8,128)(2,1)}), bf16[32,2,96,512]{3,2,1,0:T(8,128)(2,1)}) %all-gather.12.cloned.1.call-update) | async-done | bytes 6291472 | tf_op jit(solution)/shard_map/all_gather | solution.py:49
  244.3 3.4 fusion.46
  247.7 1.9 copy.88
  249.6 2.0 copy.87
  251.6 58.4 %all-gather.10.cloned.1.call-done = bf16[3072,512]{0,1:T(8,128)(2,1)} async-done(((bf16[384,512]{0,1:T(8,128)(2,1)}), bf16[3072,512]{0,1:T(8,128)(2,1)}) %all-gather.10.cloned.1.call-update) | async-done | bytes 3145744 | tf_op jit(solution)/shard_map/all_gather | solution.py:136
  310.0 5.7 %fusion.50 = f32[512,512]{1,0:T(8,128)} fusion(bf16[3072,512]{0,1:T(8,128)(2,1)} %all-gather.10.cloned.1.call-done, bf16[3072,512]{1,0:T(8,128)(2,1)} %bitcast.118), kind=kOutput, calls=%fused_computation.54 | convolution fusion | flops 1610612736 | bytes 7340032 | tf_op jit(solution)/shard_map/dot_general | solution.py:18
  315.7 76.0 %all-gather.8.cloned.1.call-done = bf16[3072,768]{0,1:T(8,128)(2,1)} async-done(((bf16[384,768]{0,1:T(8,128)(2,1)}), bf16[3072,768]{0,1:T(8,128)(2,1)}) %all-gather.8.cloned.1.call-update) | async-done | bytes 4718608 | tf_op jit(solution)/shard_map/all_gather | solution.py:138
  391.7 5.0 fusion.49
  396.7 1.1 slice.43
  397.8 0.8 fusion.47
  398.6 52.1 %reduce-scatter.3.cloned.1.call-done = f32[384,1024]{1,0:T(8,128)} async-done(((f32[384,4096]{1,0:T(8,128)}), f32[384,1024]{1,0:T(8,128)}) %reduce-scatter.3.cloned.1.call-update) | async-done | bytes 1572880 | tf_op jit(solution)/shard_map/reduce_scatter | solution.py:94
  450.7 2.4 convert_element_type.82
  453.1 58.5 %reduce-scatter.5.cloned.1.call-done = f32[384,1024]{1,0:T(8,128)} async-done(((f32[384,4096]{1,0:T(8,128)}), f32[384,1024]{1,0:T(8,128)}) %reduce-scatter.5.cloned.1.call-update) | async-done | bytes 1572880 | tf_op jit(solution)/shard_map/reduce_scatter | solution.py:133
  511.6 2.4 convert_element_type.95
  (45 shorter events, 5.4 us)
Async XLA Ops:
  7.2 8.3 %copy-start = (bf16[384,4096]{1,0:T(8,128)(2,1)S(1)}, bf16[384,4096]{1,0:T(8,128)(2,1)}, u32[]{:S(2)}) copy-start(bf16[384,4096]{1,0:T(8,128)(2,1)} %param.6) | copy-start | bytes 9437188
  7.2 190.9 %all-gather.6.cloned.1.call-start = ((), (), s32[]{:S(2)}) async-start(), calls=%async_computation.3 | async-start | bytes 11796480 | tf_op jit(solution)/shard_map/all_gather | solution.py:65
  13.9 230.4 %all-gather.12.cloned.1.call-start = ((), (), s32[]{:S(2)}) async-start(), calls=%async_computation.8 | async-start | bytes 7864320 | tf_op jit(solution)/shard_map/all_gather | solution.py:49
  98.1 211.9 %all-gather.10.cloned.1.call-start = ((), (), s32[]{:S(2)}) async-start(), calls=%async_computation.7 | async-start | bytes 3538944 | tf_op jit(solution)/shard_map/all_gather | solution.py:136
  200.4 4.6 copy-start.7
  205.5 3.3 copy-start.2
  208.8 1.4 copy-start.9
  210.2 5.7 %copy-start.3 = (f32[1,4,384,384]{2,3,1,0:T(8,128)S(1)}, f32[1,4,384,384]{2,3,1,0:T(8,128)}, u32[]{:S(2)}) copy-start(f32[1,4,384,384]{2,3,1,0:T(8,128)} %copy-done.2) | copy-start | bytes 7077892
  210.2 5.7 %copy-start.10 = (bf16[128,384,1]{1,0,2:T(8,128)(2,1)S(1)}, bf16[128,384,1]{1,0,2:T(8,128)(2,1)}, u32[]{:S(2)}) copy-start(bf16[128,384,1]{1,0,2:T(8,128)(2,1)} %copy-done.9) | copy-start | bytes 294916
  210.2 181.5 %all-gather.8.cloned.1.call-start = ((), (), s32[]{:S(2)}) async-start(), calls=%async_computation.6 | async-start | bytes 5308416 | tf_op jit(solution)/shard_map/all_gather | solution.py:138
  215.9 1.7 copy-start.4
  217.6 1.1 copy-start.8
  219.1 1.7 copy-start.6
  220.6 230.1 %reduce-scatter.3.cloned.1.call-start = ((), (), s32[]{:S(2)}) async-start(), calls=%async_computation.4 | async-start | bytes 7864320 | tf_op jit(solution)/shard_map/reduce_scatter | solution.py:94
  227.5 284.1 %reduce-scatter.5.cloned.1.call-start = ((), (), s32[]{:S(2)}) async-start(), calls=%async_computation.5 | async-start | bytes 7864320 | tf_op jit(solution)/shard_map/reduce_scatter | solution.py:133
  310.0 81.7 %copy-start.5 = (bf16[1,8,4,96,512]{4,3,2,1,0:T(8,128)(2,1)S(1)}, bf16[1,8,4,96,512]{4,3,2,1,0:T(8,128)(2,1)}, u32[]{:S(2)}) copy-start(bf16[1,8,4,96,512]{4,3,2,1,0:T(8,128)(2,1)} %copy.87) | copy-start | bytes 9437188
  397.8 116.2 %copy-start.1 = (bf16[384,4096]{1,0:T(8,128)(2,1)S(1)}, bf16[384,4096]{1,0:T(8,128)(2,1)}, u32[]{:S(2)}) copy-start(bf16[384,4096]{1,0:T(8,128)(2,1)} %param.6) | copy-start | bytes 9437188
Sparse Core Ops, SparseCore 0:
  14.0 184.0 all-gather.5
  199.7 44.5 all-gather.11
  246.9 63.0 all-gather.9
  312.5 79.1 all-gather.7
  394.1 56.5 reduce-scatter.2
  453.2 58.3 reduce-scatter.4

commit v2 on v0

--- a/solution.py
+++ b/solution.py
@@ -1,8 +1,11 @@
+import functools
 import math
 
 import jax
 import jax.numpy as jnp
 from jax import lax
+from jax.experimental import pallas as pl
+from jax.experimental.pallas import tpu as pltpu
 from jax.sharding import PartitionSpec as P
 
 HEAD_SIZE = 128
@@ -31,6 +34,204 @@
     row_max = jnp.max(scores, axis=-1, keepdims=True)
     powered = jnp.exp(scores - row_max)
     return powered / jnp.sum(powered, axis=-1, keepdims=True)
+
+
+def remote(src, dst, send, recv, dest):
+    return pltpu.make_async_remote_copy(
+        src_ref=src,
+        dst_ref=dst,
+        send_sem=send,
+        recv_sem=recv,
+        device_id={"blk": dest},
+        device_id_type=pl.DeviceIdType.MESH,
+    )
+
+
+def greet(n):
+    me = lax.axis_index("blk")
+    barrier = pltpu.get_barrier_semaphore()
+    for offset in range(1, n):
+        pl.semaphore_signal(
+            barrier,
+            inc=1,
+            device_id={"blk": lax.rem(me + offset, n)},
+            device_id_type=pl.DeviceIdType.MESH,
+        )
+    pl.semaphore_wait(barrier, n - 1)
+
+
+def chain_gather(n, own, out, chain_send, chain_recv, side_send, side_recv, own_sem):
+    me = lax.axis_index("blk")
+    length = n // 2
+    place, side = me // 2, lax.rem(me, 2)
+    other = place * 2 + (1 - side)
+
+    def along(way, origin, first):
+        src = own if first else out.at[origin * 2 + side]
+        step = 2 if way == 0 else -2
+        return remote(
+            src, out.at[origin * 2 + side], chain_send.at[way, origin], chain_recv.at[origin], me + step
+        )
+
+    def across(origin, first):
+        src = own if first else out.at[origin * 2 + side]
+        return remote(
+            src, out.at[origin * 2 + side], side_send.at[origin], side_recv.at[origin], other
+        )
+
+    can = (place + 1 < length, place >= 1)
+    for way in range(2):
+        @pl.when(can[way])
+        def _():
+            along(way, place, True).start()
+
+    across(place, True).start()
+    mine = pltpu.make_async_copy(own, out.at[me], own_sem)
+    mine.start()
+    for step in range(1, length):
+        for way in range(2):
+            origin = place - step if way == 0 else place + step
+            there = origin >= 0 if way == 0 else origin < length
+
+            @pl.when(there)
+            def _():
+                along(way, origin, False).wait_recv()
+
+            @pl.when(jnp.logical_and(there, can[way]))
+            def _():
+                along(way, origin, False).start()
+
+            @pl.when(there)
+            def _():
+                across(origin, False).start()
+
+    def finish():
+        mine.wait()
+        for step in range(length):
+            for way in range(2):
+                if step == 0 and way == 1:
+                    continue
+                origin = place - step if way == 0 else place + step
+                there = origin >= 0 if way == 0 else origin < length
+
+                @pl.when(there)
+                def _():
+                    across(origin, step == 0).wait_send()
+
+            for way in range(2):
+                origin = place - step if way == 0 else place + step
+                there = origin >= 0 if way == 0 else origin < length
+
+                @pl.when(jnp.logical_and(there, can[way]))
+                def _():
+                    along(way, origin, step == 0).wait_send()
+
+        for origin in range(length):
+            landed = out.at[origin * 2 + (1 - side)]
+            remote(landed, landed, side_send.at[origin], side_recv.at[origin], other).wait_recv()
+
+    return finish
+
+
+def gather_semaphores(n):
+    length = n // 2
+    return [
+        pltpu.SemaphoreType.DMA((2, length)),
+        pltpu.SemaphoreType.DMA((length,)),
+        pltpu.SemaphoreType.DMA((length,)),
+        pltpu.SemaphoreType.DMA((length,)),
+        pltpu.SemaphoreType.DMA,
+    ]
+
+
+def first_kernel(n, parts, weights, tokens, out_grad, out, landed, *sems):
+    gather_sems, (part_send, part_recv, part_own) = sems[:5], sems[5:]
+    me = lax.axis_index("blk")
+    rows = tokens.shape[0] // parts
+    cols = tokens.shape[1] // n
+    first = pl.multiple_of(lax.axis_index("tp") * rows, rows)
+    greet(n)
+
+    def part(which, dest):
+        at = pl.multiple_of(dest * cols, cols)
+        return (tokens, out_grad)[which].at[pl.ds(first, rows), pl.ds(at, cols)]
+
+    def sending(which, offset):
+        dest = lax.rem(me + offset, n)
+        return remote(
+            part(which, dest),
+            landed.at[which, me],
+            part_send.at[which, offset],
+            part_recv.at[which, offset],
+            dest,
+        )
+
+    own_parts = [
+        pltpu.make_async_copy(part(which, me), landed.at[which, me], part_own.at[which])
+        for which in range(2)
+    ]
+    for copy in own_parts:
+        copy.start()
+    for which in range(2):
+        for offset in range(1, n):
+            sending(which, offset).start()
+    finish = chain_gather(n, weights, out, *gather_sems)
+    finish()
+    for copy in own_parts:
+        copy.wait()
+    for which in range(2):
+        for offset in range(1, n):
+            sending(which, offset).wait_send()
+            origin = lax.rem(me + n - offset, n)
+            here = landed.at[which, origin]
+            remote(
+                here, here, part_send.at[which, offset], part_recv.at[which, offset], origin
+            ).wait_recv()
+
+
+def second_kernel(n, own, out, *sems):
+    greet(n)
+    chain_gather(n, own, out, *sems)()
+
+
+def gather_inputs(weights, tokens, out_grad, tp_count, n):
+    rows = tokens.shape[0] // tp_count
+    cols = tokens.shape[1] // n
+    anywhere = pl.BlockSpec(memory_space=pl.ANY)
+    gathered, landed = pl.pallas_call(
+        functools.partial(first_kernel, n, tp_count),
+        out_shape=(
+            jax.ShapeDtypeStruct((n,) + weights.shape, weights.dtype),
+            jax.ShapeDtypeStruct((2, n, rows, cols), tokens.dtype),
+        ),
+        in_specs=[anywhere] * 3,
+        out_specs=(anywhere, anywhere),
+        scratch_shapes=gather_semaphores(n)
+        + [
+            pltpu.SemaphoreType.DMA((2, n)),
+            pltpu.SemaphoreType.DMA((2, n)),
+            pltpu.SemaphoreType.DMA((2,)),
+        ],
+        compiler_params=pltpu.CompilerParams(collective_id=0, has_side_effects=True),
+        cost_estimate=pl.CostEstimate(flops=0, bytes_accessed=300_000_000, transcendentals=0),
+        name="gather_inputs",
+    )(weights, tokens, out_grad)
+    return gathered.reshape(n * weights.shape[0], weights.shape[1]), landed
+
+
+def gather_grads(own, n):
+    anywhere = pl.BlockSpec(memory_space=pl.ANY)
+    gathered = pl.pallas_call(
+        functools.partial(second_kernel, n),
+        out_shape=jax.ShapeDtypeStruct((n,) + own.shape, own.dtype),
+        in_specs=[anywhere],
+        out_specs=anywhere,
+        scratch_shapes=gather_semaphores(n),
+        compiler_params=pltpu.CompilerParams(collective_id=1, has_side_effects=True),
+        cost_estimate=pl.CostEstimate(flops=0, bytes_accessed=250_000_000, transcendentals=0),
+        name="gather_grads",
+    )(own)
+    return gathered.reshape(n * own.shape[0], own.shape[1])
 
 
 def on_device(tokens, w_query, key_weight, value_weight, w_output, out_grad):
@@ -41,15 +242,22 @@
     group_width = head_cols // kv_cols
     block_count = sequence_length // sequence_length
     score_scale = 1.0 / math.sqrt(HEAD_SIZE)
-    output_rows = lax.all_gather(w_output, "blk", axis=1, tiled=True)
-    query_rows, key_rows, value_rows = (
-        lax.all_gather(w_query, "blk", axis=0, tiled=True),
-        lax.all_gather(key_weight, "blk", axis=0, tiled=True),
-        lax.all_gather(value_weight, "blk", axis=0, tiled=True),
-    )
-    query_full = jnp.dot(tokens, query_rows, preferred_element_type=jnp.float32)
-    key_full = jnp.dot(tokens, key_rows, preferred_element_type=jnp.float32)
-    value_full = jnp.dot(tokens, value_rows, preferred_element_type=jnp.float32)
+    tp_count = lax.axis_size("tp")
+    blk_count = lax.axis_size("blk")
+    weight_block = jnp.concatenate([w_query, key_weight, value_weight, w_output.T], axis=1)
+    weight_rows, landed = gather_inputs(weight_block, tokens, out_grad, tp_count, blk_count)
+    joint_cols = head_cols + 2 * kv_cols
+    joint_rows = weight_rows[:, :joint_cols]
+    output_cols = weight_rows[:, joint_cols:]
+    block_cols = landed.shape[3]
+    inputs_by_cols = lax.all_gather(landed, "tp", axis=0)
+    inputs_by_cols = jnp.transpose(inputs_by_cols, (1, 2, 0, 3, 4)).reshape(
+        2, blk_count * sequence_length, block_cols
+    )
+    joint_full = jnp.dot(tokens, joint_rows, preferred_element_type=jnp.float32)
+    query_full = joint_full[:, :head_cols]
+    key_full = joint_full[:, head_cols : head_cols + kv_cols]
+    value_full = joint_full[:, head_cols + kv_cols :]
     query_activation = query_full.astype(jnp.bfloat16)
     query_head_rows = query_activation.reshape(sequence_length, local_kv, group_width, HEAD_SIZE)
     key_activation = key_full.astype(jnp.bfloat16)
@@ -69,12 +277,12 @@
 
     ignored_carry, mix_blocks = lax.scan(forward_block, jnp.zeros((), jnp.int32), block_ids)
     head_mix = mix_blocks.reshape(sequence_length, head_cols)
-    out_term = jnp.dot(head_mix, output_rows, preferred_element_type=jnp.float32)
+    out_term = transposed_product(head_mix, output_cols)
     attn_out = lax.psum_scatter(out_term, "tp", scatter_dimension=1, tiled=True).astype(
         jnp.bfloat16
     )
     heads_gradient = (
-        transposed_product(out_grad, output_rows)
+        jnp.dot(out_grad, output_cols, preferred_element_type=jnp.float32)
         .astype(jnp.bfloat16)
         .reshape(sequence_length, local_kv, group_width, HEAD_SIZE)
     )
@@ -104,23 +312,18 @@
     grad_query = query_blocks.reshape(sequence_length, head_cols)
     key_gradient = kv_totals[0].astype(jnp.bfloat16).reshape(sequence_length, kv_cols)
     value_gradient = kv_totals[1].astype(jnp.bfloat16).reshape(sequence_length, kv_cols)
-    input_term = (
-        transposed_product(grad_query, query_rows)
-        + transposed_product(key_gradient, key_rows)
-        + transposed_product(value_gradient, value_rows)
-    )
+    joined_grads = jnp.concatenate([grad_query, key_gradient, value_gradient], axis=1)
+    input_term = transposed_product(joined_grads, joint_rows)
     tokens_grad = lax.psum_scatter(input_term, "tp", scatter_dimension=1, tiled=True).astype(
         jnp.bfloat16
     )
-    joined_grads = jnp.concatenate([grad_query, key_gradient, value_gradient], axis=1)
-    joint_grad = lax.psum_scatter(
-        leading_product(tokens, joined_grads), "blk", scatter_dimension=0, tiled=True
-    )
+    grads_all = gather_grads(jnp.concatenate([joined_grads, head_mix], axis=1), blk_count)
+    tokens_cols, out_grad_cols = inputs_by_cols[0], inputs_by_cols[1]
+    joint_grad = leading_product(tokens_cols, grads_all[:, :joint_cols])
     query_grad = joint_grad[:, :head_cols]
     key_grad = joint_grad[:, head_cols : head_cols + kv_cols]
     value_grad = joint_grad[:, head_cols + kv_cols :]
-    output_term = leading_product(head_mix, out_grad)
-    output_grad = lax.psum_scatter(output_term, "blk", scatter_dimension=1, tiled=True)
+    output_grad = leading_product(grads_all[:, joint_cols:], out_grad_cols)
     return (attn_out, tokens_grad, query_grad, key_grad, value_grad, output_grad)
 
 

time: 740 us -> 344 us (0.46)
  waiting for transfers between devices: 651 us -> 21.4 us
  Pallas kernels: 0 us -> 245 us
  matrix products: 50.9 us -> 40.2 us
    reduce_scatter x2 -> x0, waiting for transfers between devices: 352 us -> none  [the longest x1 209 us: on_device(): lax.psum_scatter(leading_product(tokens, joined_grads), 'blk', scatter_di...]
    pallas_call x0 -> x2, Pallas kernels: none -> 245 us  [the longest x1 157 us: gather_inputs(): pl.pallas_call(functools.partial(first_kernel, n, tp_count), out_shape=(j...]
    all_gather x4 -> x1, waiting for transfers between devices: 218 us -> 0.02 us  [on_device(): inputs_by_cols = lax.all_gather(landed, 'tp', axis=0)]
    reduce_scatter x1, waiting for transfers between devices: 58.5 us -> 21.3 us  [on_device(): lax.psum_scatter(input_term, 'tp', scatter_dimension=1, tiled=True)]
    reduce_scatter x1, waiting for transfers between devices: 19 us -> 0.01 us  [on_device(): lax.psum_scatter(out_term, 'tp', scatter_dimension=1, tiled=True)]
    dot_general x2, matrix products: 14.8 us -> 5.43 us  [leading_product(): lax.dot_general(first_operand, second_operand, (((0,), (0,)), ((), ())),...]
    dot_general x4 -> x2, matrix products: 17.1 us -> 11.2 us  [the longest x1 5.66 us: on_device(): joint_full = jnp.dot(tokens, joint_rows, preferred_element_type=jnp.float32)]
    dot_general x4 -> x2, matrix products: 12.3 us -> 15.8 us  [transposed_product(): lax.dot_general(first_operand, second_operand, (((1,), (1,)), ((), ())),...]
  transfers between devices with their start and end apart: 8 -> 3, of which waited for: 8 -> 1; matrix products, arithmetic and copies ran while one was open for 8% -> 15% of each run, Pallas kernels for 0% -> 26%
where the time goes in v2:
time: 344 us
  Pallas kernels  245 us (71%)
  matrix products  40.2 us (12%)
  waiting for transfers between devices  21.4 us (6%)
  between operations  14 us (4%)
  local copies, waits for them, and re-layouts  13.4 us (4%)
  other arithmetic  9.14 us (3%)
    pallas_call x1, Pallas kernels, gather_inputs(): pl.pallas_call(functools.partial(first_kernel, n, tp_count), out_shape=(j...  157 us
    pallas_call x1, Pallas kernels, gather_grads(): pl.pallas_call(functools.partial(second_kernel, n), out_shape=jax.ShapeDt...  88.2 us
    reduce_scatter x1, waiting for transfers between devices, on_device(): lax.psum_scatter(input_term, 'tp', scatter_dimension=1, tiled=True)  21.3 us
    dot_general x2, matrix products, transposed_product(): lax.dot_general(first_operand, second_operand, (((1,), (1,)), ((), ())),...  15.8 us
  transfers between devices with their start and end apart: 3, of which 1 were waited for; matrix products, arithmetic and copies ran while one was open for 15% of the time, Pallas kernels for 26%

profile of v2, /device:TPU:0, one launch (start us, length us, event | category | flops | bytes accessed | tf_op | source)
XLA Modules:
  0.0 343.6 jit_solution(2190163836169213884)
XLA Ops:
  7.2 1.3 copy.52
  8.5 2.4 pad_maximum_fusion.weights
  10.8 157.0 %gather_inputs.1 = (bf16[8,512,1280]{2,1,0:T(8,128)(2,1)}, bf16[2,8,96,512]{3,2,1,0:T(8,128)(2,1)}) custom-call(bf16[512,1280]{1,0:T(8,128)(2,1)} %pad_maximum_fusion.weights, bf16[384,4096]{1,0:T(8,128)(2,1)} %tokens.1, bf16[384,4096]{1,0:T(8,128)(2,1)} %out_grad.1), custom_call_target="tpu_custom_call" | custom-call | bytes 300000000 | tf_op jit(solution)/shard_map/gather_inputs/pallas_call | solution.py:201
  167.9 5.7 %fusion.21 = bf16[384,768]{0,1:T(8,128)(2,1)S(1)} fusion(bf16[384,4096]{1,0:T(8,128)(2,1)S(1)} %copy-done.1, bf16[4096,1280]{1,0:T(8,128)(2,1)} %bitcast.111), kind=kOutput, calls=%fused_computation.25 | convolution fusion | flops 2416214016 | bytes 10027008 | tf_op jit(solution)/shard_map/dot_general | solution.py:257
  173.6 0.8 copy-done.2
  174.5 0.5 fusion.55
  175.0 0.3 fusion.17
  175.3 0.6 convolution_convert_fusion.1
  175.9 0.7 copy-done.4
  176.7 6.9 %fusion.8 = f32[384,4096]{1,0:T(8,128)} fusion(bf16[384,512]{0,1:T(8,128)(2,1)S(1)} %bitcast.118, bf16[4096,1280]{1,0:T(8,128)(2,1)} %bitcast.112), kind=kOutput, calls=%fused_computation.8 | convolution fusion | flops 1610612736 | bytes 10878976 | tf_op jit(solution)/shard_map/dot_general | solution.py:15
  183.8 5.6 %fusion.24 = bf16[512,384]{1,0:T(8,128)(2,1)S(1)} fusion(bf16[384,4096]{1,0:T(8,128)(2,1)} %out_grad.1, bf16[4096,1280]{1,0:T(8,128)(2,1)} %bitcast.113), kind=kOutput, calls=%fused_computation.28 | convolution fusion | flops 1610809344 | bytes 7733248 | tf_op jit(solution)/shard_map/dot_general | solution.py:285
  189.4 1.6 fusion.12
  191.0 0.6 fusion.27
  191.7 2.0 convolution_convert_fusion
  193.7 1.9 copy.80
  195.6 1.5 fusion.41
  197.1 1.6 fusion.38
  198.7 8.9 %fusion = f32[384,4096]{1,0:T(8,128)} fusion(bf16[4096,1280]{1,0:T(8,128)(2,1)} %bitcast.114, bf16[384,128]{1,0:T(8,128)(2,1)S(1)} %fusion.38, bf16[384,128]{1,0:T(8,128)(2,1)S(1)} %fusion.41, bf16[384,512]{1,0:T(8,128)(2,1)S(1)} %copy-done.3), kind=kOutput, calls=%fused_computation | convolution fusion | flops 2417688576 | bytes 13172736 | tf_op jit(solution)/shard_map/dot_general | solution.py:15
  207.6 1.0 copy-done.5
  208.8 1.0 pad_maximum_fusion.1.own
  209.8 88.2 %gather_grads.1 = bf16[8,384,1280]{2,1,0:T(8,128)(2,1)} custom-call(bf16[384,1280]{1,0:T(8,128)(2,1)} %pad_maximum_fusion.1.own), custom_call_target="tpu_custom_call" | custom-call | bytes 250000000 | tf_op jit(solution)/shard_map/gather_grads/pallas_call | solution.py:224
  298.0 3.6 %fusion.53 = (bf16[1,8,4,96,512]{4,3,1,0,2:T(8,128)(2,1)S(1)}, bf16[1,8,4,96,512]{4,3,1,0,2:T(8,128)(2,1)S(1)}) fusion(bf16[2,8,4,96,512]{4,3,1,0,2:T(8,128)(2,1)} %bitcast.107), kind=kLoop, calls=%fused_computation.51 | loop fusion | bytes 12582912 | tf_op jit(solution)/shard_map/slice | solution.py:321
  301.6 0.3 copy.65
  301.9 1.4 copy-done
  303.3 2.6 fusion.4
  305.9 1.1 slice.60
  307.1 0.2 copy.66
  307.3 0.8 fusion.54
  308.1 2.8 fusion.10
  310.9 2.4 convert_element_type.67
  313.3 21.3 %reduce-scatter.5.cloned.1.call-done = f32[384,1024]{1,0:T(8,128)} async-done(((f32[384,4096]{1,0:T(8,128)}), f32[384,1024]{1,0:T(8,128)}) %reduce-scatter.5.cloned.1.call-update) | async-done | bytes 1572880 | tf_op jit(solution)/shard_map/reduce_scatter | solution.py:317
  334.7 2.4 convert_element_type.80
  (26 shorter events, 0.6 us)
Async XLA Ops:
  7.2 290.9 %all-gather.3.cloned.1.call-start = ((), (), s32[]{:S(2)}) async-start(), calls=%async_computation.4 | async-start | bytes 7864320 | tf_op jit(solution)/shard_map/all_gather | solution.py:253
  10.8 157.1 %copy-start.1 = (bf16[384,4096]{1,0:T(8,128)(2,1)S(1)}, bf16[384,4096]{1,0:T(8,128)(2,1)}, u32[]{:S(2)}) copy-start(bf16[384,4096]{1,0:T(8,128)(2,1)} %tokens.1) | copy-start | bytes 9437188
  167.8 143.1 %reduce-scatter.3.cloned.1.call-start = ((), (), s32[]{:S(2)}) async-start(), calls=%async_computation.2 | async-start | bytes 7864320 | tf_op jit(solution)/shard_map/reduce_scatter | solution.py:281
  173.6 1.7 copy-start.6
  173.6 0.8 copy-start.2
  175.9 0.8 copy-start.4
  183.6 151.1 %reduce-scatter.5.cloned.1.call-start = ((), (), s32[]{:S(2)}) async-start(), calls=%async_computation.3 | async-start | bytes 7864320 | tf_op jit(solution)/shard_map/reduce_scatter | solution.py:317
  189.4 1.7 copy-start.9
  197.0 1.6 copy-start.7
  197.1 1.6 copy-start.3
  207.5 1.0 copy-start.5
  207.6 1.2 copy-start.8
  298.0 5.3 %copy-start = (bf16[8,384,1280]{2,1,0:T(8,128)(2,1)S(1)}, bf16[8,384,1280]{2,1,0:T(8,128)(2,1)}, u32[]{:S(2)}) copy-start(bf16[8,384,1280]{2,1,0:T(8,128)(2,1)} %gather_grads.1) | copy-start | bytes 23592964
Sparse Core Ops, SparseCore 0:
  168.0 44.6 all-gather.2
  215.2 58.3 reduce-scatter.2
  276.3 58.3 reduce-scatter.4

commit v3 on v2

--- a/solution.py
+++ b/solution.py
@@ -36,18 +36,18 @@
     return powered / jnp.sum(powered, axis=-1, keepdims=True)
 
 
-def remote(src, dst, send, recv, dest):
+def remote(src, dst, send, recv, dest, axis="blk"):
     return pltpu.make_async_remote_copy(
         src_ref=src,
         dst_ref=dst,
         send_sem=send,
         recv_sem=recv,
-        device_id={"blk": dest},
+        device_id={axis: dest},
         device_id_type=pl.DeviceIdType.MESH,
     )
 
 
-def greet(n):
+def greet(n, parts=1):
     me = lax.axis_index("blk")
     barrier = pltpu.get_barrier_semaphore()
     for offset in range(1, n):
@@ -57,10 +57,18 @@
             device_id={"blk": lax.rem(me + offset, n)},
             device_id_type=pl.DeviceIdType.MESH,
         )
-    pl.semaphore_wait(barrier, n - 1)
-
-
-def chain_gather(n, own, out, chain_send, chain_recv, side_send, side_recv, own_sem):
+    mate = lax.axis_index("tp")
+    for offset in range(1, parts):
+        pl.semaphore_signal(
+            barrier,
+            inc=1,
+            device_id={"tp": lax.rem(mate + offset, parts)},
+            device_id_type=pl.DeviceIdType.MESH,
+        )
+    pl.semaphore_wait(barrier, n - 1 + parts - 1)
+
+
+def chain_gather(n, own, out, chain_send, chain_recv, side_send, side_recv, own_sem, begin=None, between=None):
     me = lax.axis_index("blk")
     length = n // 2
     place, side = me // 2, lax.rem(me, 2)
@@ -85,6 +93,8 @@
         def _():
             along(way, place, True).start()
 
+    if begin is not None:
+        begin()
     across(place, True).start()
     mine = pltpu.make_async_copy(own, out.at[me], own_sem)
     mine.start()
@@ -104,6 +114,9 @@
             @pl.when(there)
             def _():
                 across(origin, False).start()
+
+        if between is not None:
+            between(step)
 
     def finish():
         mine.wait()
@@ -145,12 +158,13 @@
 
 
 def first_kernel(n, parts, weights, tokens, out_grad, out, landed, *sems):
-    gather_sems, (part_send, part_recv, part_own) = sems[:5], sems[5:]
+    gather_sems, (part_send, part_recv, part_own, mate_send, mate_recv) = sems[:5], sems[5:]
     me = lax.axis_index("blk")
+    mate = lax.axis_index("tp")
     rows = tokens.shape[0] // parts
     cols = tokens.shape[1] // n
-    first = pl.multiple_of(lax.axis_index("tp") * rows, rows)
-    greet(n)
+    first = pl.multiple_of(mate * rows, rows)
+    greet(n, parts)
 
     def part(which, dest):
         at = pl.multiple_of(dest * cols, cols)
@@ -160,33 +174,66 @@
         dest = lax.rem(me + offset, n)
         return remote(
             part(which, dest),
-            landed.at[which, me],
+            landed.at[which, me, mate],
             part_send.at[which, offset],
             part_recv.at[which, offset],
             dest,
         )
 
+    def arriving(which, offset):
+        origin = lax.rem(me + n - offset, n)
+        here = landed.at[which, origin, mate]
+        return remote(here, here, part_send.at[which, offset], part_recv.at[which, offset], origin)
+
+    def sharing(offset, other):
+        here = landed.at[:, lax.rem(me + n - offset, n), mate]
+        dest = lax.rem(mate + other, parts)
+        return remote(here, here, mate_send.at[offset, other], mate_recv.at[offset, other], dest, "tp")
+
+    def shared(offset, other):
+        source = lax.rem(mate + parts - other, parts)
+        here = landed.at[:, lax.rem(me + n - offset, n), source]
+        return remote(here, here, mate_send.at[offset, other], mate_recv.at[offset, other], source, "tp")
+
     own_parts = [
-        pltpu.make_async_copy(part(which, me), landed.at[which, me], part_own.at[which])
+        pltpu.make_async_copy(part(which, me), landed.at[which, me, mate], part_own.at[which])
         for which in range(2)
     ]
-    for copy in own_parts:
-        copy.start()
-    for which in range(2):
+    steps = n // 2 - 1
+    share = -(-(n - 1) // max(steps, 1))
+
+    def begin():
+        for copy in own_parts:
+            copy.start()
         for offset in range(1, n):
-            sending(which, offset).start()
-    finish = chain_gather(n, weights, out, *gather_sems)
+            for which in range(2):
+                sending(which, offset).start()
+        for copy in own_parts:
+            copy.wait()
+        for other in range(1, parts):
+            sharing(0, other).start()
+
+    def pass_on(offsets):
+        for offset in offsets:
+            for which in range(2):
+                arriving(which, offset).wait_recv()
+            for other in range(1, parts):
+                sharing(offset, other).start()
+
+    def between(step):
+        pass_on(range(1 + (step - 1) * share, min(1 + step * share, n)))
+
+    finish = chain_gather(n, weights, out, *gather_sems, begin=begin, between=between)
+    if steps == 0:
+        pass_on(range(1, n))
     finish()
-    for copy in own_parts:
-        copy.wait()
-    for which in range(2):
-        for offset in range(1, n):
+    for offset in range(1, n):
+        for which in range(2):
             sending(which, offset).wait_send()
-            origin = lax.rem(me + n - offset, n)
-            here = landed.at[which, origin]
-            remote(
-                here, here, part_send.at[which, offset], part_recv.at[which, offset], origin
-            ).wait_recv()
+    for offset in range(n):
+        for other in range(1, parts):
+            sharing(offset, other).wait_send()
+            shared(offset, other).wait_recv()
 
 
 def second_kernel(n, own, out, *sems):
@@ -202,7 +249,7 @@
         functools.partial(first_kernel, n, tp_count),
         out_shape=(
             jax.ShapeDtypeStruct((n,) + weights.shape, weights.dtype),
-            jax.ShapeDtypeStruct((2, n, rows, cols), tokens.dtype),
+            jax.ShapeDtypeStruct((2, n, tp_count, rows, cols), tokens.dtype),
         ),
         in_specs=[anywhere] * 3,
         out_specs=(anywhere, anywhere),
@@ -211,6 +258,8 @@
             pltpu.SemaphoreType.DMA((2, n)),
             pltpu.SemaphoreType.DMA((2, n)),
             pltpu.SemaphoreType.DMA((2,)),
+            pltpu.SemaphoreType.DMA((n, tp_count)),
+            pltpu.SemaphoreType.DMA((n, tp_count)),
         ],
         compiler_params=pltpu.CompilerParams(collective_id=0, has_side_effects=True),
         cost_estimate=pl.CostEstimate(flops=0, bytes_accessed=300_000_000, transcendentals=0),
@@ -249,11 +298,7 @@
     joint_cols = head_cols + 2 * kv_cols
     joint_rows = weight_rows[:, :joint_cols]
     output_cols = weight_rows[:, joint_cols:]
-    block_cols = landed.shape[3]
-    inputs_by_cols = lax.all_gather(landed, "tp", axis=0)
-    inputs_by_cols = jnp.transpose(inputs_by_cols, (1, 2, 0, 3, 4)).reshape(
-        2, blk_count * sequence_length, block_cols
-    )
+    inputs_by_cols = landed.reshape(2, blk_count * sequence_length, landed.shape[4])
     joint_full = jnp.dot(tokens, joint_rows, preferred_element_type=jnp.float32)
     query_full = joint_full[:, :head_cols]
     key_full = joint_full[:, head_cols : head_cols + kv_cols]

time: 344 us -> 321 us (0.933)
  waiting for transfers between devices: 21.4 us -> 0.04 us
    reduce_scatter x1, waiting for transfers between devices: 21.3 us -> 0.01 us  [on_device(): lax.psum_scatter(input_term, 'tp', scatter_dimension=1, tiled=True)]
  transfers between devices with their start and end apart: 3 -> 2, of which waited for: 1 -> 0; matrix products, arithmetic and copies ran while one was open for 15% -> 12% of each run, Pallas kernels for 26% -> 27%
where the time goes in v3:
time: 321 us; the launch traced here: 320 us
  Pallas kernels  243 us (76%)
  matrix products  40.5 us (13%)
  between operations  14.2 us (4%)
  local copies, waits for them, and re-layouts  13.1 us (4%)
  other arithmetic  9.13 us (3%)
    pallas_call x1, Pallas kernels, gather_inputs(): pl.pallas_call(functools.partial(first_kernel, n, tp_count), out_shape=(j...  157 us
    pallas_call x1, Pallas kernels, gather_grads(): pl.pallas_call(functools.partial(second_kernel, n), out_shape=jax.ShapeDt...  85.7 us
    dot_general x2, matrix products, transposed_product(): lax.dot_general(first_operand, second_operand, (((1,), (1,)), ((), ())),...  15.5 us
    dot_general x1, matrix products, on_device(): joint_full = jnp.dot(tokens, joint_rows, preferred_element_type=jnp.float32)  7.16 us
  transfers between devices with their start and end apart: 2, of which 0 were waited for; matrix products, arithmetic and copies ran while one was open for 12% of the time, Pallas kernels for 27%

profile of v3, /device:TPU:0, one launch (start us, length us, event | category | flops | bytes accessed | tf_op | source)
XLA Modules:
  0.0 320.1 jit_solution(528272797470516108)
XLA Ops:
  7.2 1.3 copy.12
  8.5 2.4 pad_maximum_fusion.weights
  10.8 157.1 %gather_inputs.1 = (bf16[8,512,1280]{2,1,0:T(8,128)(2,1)}, bf16[2,8,4,96,512]{4,3,2,1,0:T(8,128)(2,1)}) custom-call(bf16[512,1280]{1,0:T(8,128)(2,1)} %pad_maximum_fusion.weights, bf16[384,4096]{1,0:T(8,128)(2,1)} %tokens.1, bf16[384,4096]{1,0:T(8,128)(2,1)} %out_grad.1), custom_call_target="tpu_custom_call" | custom-call | bytes 300000000 | tf_op jit(solution)/shard_map/gather_inputs/pallas_call | solution.py:248
  167.9 7.2 %fusion.21 = bf16[384,768]{0,1:T(8,128)(2,1)S(1)} fusion(bf16[384,4096]{1,0:T(8,128)(2,1)} %tokens.1, bf16[4096,1280]{1,0:T(8,128)(2,1)} %bitcast.107), kind=kOutput, calls=%fused_computation.25 | convolution fusion | flops 2416214016 | bytes 10027008 | tf_op jit(solution)/shard_map/dot_general | solution.py:302
  175.2 0.8 copy-done.1
  176.0 0.5 fusion.55
  176.5 0.3 fusion.17
  176.9 0.6 convolution_convert_fusion.1
  177.5 0.7 copy-done.3
  178.2 6.7 %fusion.8 = f32[384,4096]{1,0:T(8,128)} fusion(bf16[384,512]{0,1:T(8,128)(2,1)S(1)} %bitcast.114, bf16[4096,1280]{1,0:T(8,128)(2,1)} %bitcast.108), kind=kOutput, calls=%fused_computation.8 | convolution fusion | flops 1610612736 | bytes 10878976 | tf_op jit(solution)/shard_map/dot_general | solution.py:15
  184.9 0.2 reduce-scatter.5.cloned.1.call-start
  185.2 5.6 %fusion.24 = bf16[512,384]{1,0:T(8,128)(2,1)S(1)} fusion(bf16[384,4096]{1,0:T(8,128)(2,1)} %out_grad.1, bf16[4096,1280]{1,0:T(8,128)(2,1)} %bitcast.109), kind=kOutput, calls=%fused_computation.28 | convolution fusion | flops 1610809344 | bytes 7733248 | tf_op jit(solution)/shard_map/dot_general | solution.py:330
  190.8 0.6 fusion.12
  191.4 0.1 copy-done.8
  191.5 0.6 fusion.27
  192.1 2.1 convolution_convert_fusion
  194.2 1.9 copy.38
  196.1 1.5 fusion.41
  197.6 1.6 fusion.38
  199.2 8.8 %fusion = f32[384,4096]{1,0:T(8,128)} fusion(bf16[4096,1280]{1,0:T(8,128)(2,1)} %bitcast.110, bf16[384,128]{1,0:T(8,128)(2,1)S(1)} %fusion.38, bf16[384,128]{1,0:T(8,128)(2,1)S(1)} %fusion.41, bf16[384,512]{1,0:T(8,128)(2,1)S(1)} %copy-done.2), kind=kOutput, calls=%fused_computation | convolution fusion | flops 2417688576 | bytes 13172736 | tf_op jit(solution)/shard_map/dot_general | solution.py:15
  208.0 1.0 copy-done.4
  209.0 0.2 copy.36
  209.2 1.0 pad_maximum_fusion.1.own
  210.2 85.7 %gather_grads.1 = bf16[8,384,1280]{2,1,0:T(8,128)(2,1)} custom-call(bf16[384,1280]{1,0:T(8,128)(2,1)} %pad_maximum_fusion.1.own), custom_call_target="tpu_custom_call" | custom-call | bytes 250000000 | tf_op jit(solution)/shard_map/gather_grads/pallas_call | solution.py:273
  296.0 3.5 %fusion.53 = (bf16[1,8,4,96,512]{4,3,2,1,0:T(8,128)(2,1)S(1)}, bf16[1,8,4,96,512]{4,3,2,1,0:T(8,128)(2,1)S(1)}) fusion(bf16[2,8,4,96,512]{4,3,2,1,0:T(8,128)(2,1)} %get-tuple-element.40), kind=kLoop, calls=%fused_computation.51 | loop fusion | bytes 12582912 | tf_op jit(solution)/shard_map/slice | solution.py:366
  299.4 1.6 copy-done
  301.0 2.6 fusion.4
  303.7 1.1 slice.59
  304.8 0.8 fusion.54
  305.6 2.8 fusion.10
  308.4 2.4 convert_element_type.67
  310.8 2.4 convert_element_type.80
  (19 shorter events, 0.2 us)
Async XLA Ops:
  7.2 301.3 %reduce-scatter.3.cloned.1.call-start = ((), (), s32[]{:S(2)}) async-start(), calls=%async_computation.2 | async-start | bytes 7864320 | tf_op jit(solution)/shard_map/reduce_scatter | solution.py:326
  175.1 15.6 %copy-start.5 = (bf16[384,768]{0,1:T(8,128)(2,1)}, bf16[384,768]{0,1:T(8,128)(2,1)S(1)}, u32[]{:S(2)}) copy-start(bf16[384,768]{0,1:T(8,128)(2,1)S(1)} %fusion.21) | copy-start | bytes 1769476
  175.2 0.8 copy-start.1
  177.4 0.8 copy-start.3
  184.9 125.9 %reduce-scatter.5.cloned.1.call-start = ((), (), s32[]{:S(2)}) async-start(), calls=%async_computation.3 | async-start | bytes 7864320 | tf_op jit(solution)/shard_map/reduce_scatter | solution.py:362
  190.7 0.7 copy-start.8
  197.6 1.6 copy-start.6
  197.6 1.6 copy-start.2
  208.0 1.0 copy-start.4
  208.0 1.2 copy-start.7
  296.0 5.1 %copy-start = (bf16[8,384,1280]{2,1,0:T(8,128)(2,1)S(1)}, bf16[8,384,1280]{2,1,0:T(8,128)(2,1)}, u32[]{:S(2)}) copy-start(bf16[8,384,1280]{2,1,0:T(8,128)(2,1)} %gather_grads.1) | copy-start | bytes 23592964
Sparse Core Ops, SparseCore 0:
  185.1 56.6 reduce-scatter.2
  244.4 58.3 reduce-scatter.4

commit v4 on v3

--- a/solution.py
+++ b/solution.py
@@ -93,9 +93,9 @@
         def _():
             along(way, place, True).start()
 
+    across(place, True).start()
     if begin is not None:
         begin()
-    across(place, True).start()
     mine = pltpu.make_async_copy(own, out.at[me], own_sem)
     mine.start()
     for step in range(1, length):
@@ -157,7 +157,8 @@
     ]
 
 
-def first_kernel(n, parts, weights, tokens, out_grad, out, landed, *sems):
+def first_kernel(n, parts, weights, tokens, out_grad, out, landed_tokens, landed_grad, *sems):
+    landed = (landed_tokens, landed_grad)
     gather_sems, (part_send, part_recv, part_own, mate_send, mate_recv) = sems[:5], sems[5:]
     me = lax.axis_index("blk")
     mate = lax.axis_index("tp")
@@ -174,7 +175,7 @@
         dest = lax.rem(me + offset, n)
         return remote(
             part(which, dest),
-            landed.at[which, me, mate],
+            landed[which].at[me, mate],
             part_send.at[which, offset],
             part_recv.at[which, offset],
             dest,
@@ -182,25 +183,24 @@
 
     def arriving(which, offset):
         origin = lax.rem(me + n - offset, n)
-        here = landed.at[which, origin, mate]
+        here = landed[which].at[origin, mate]
         return remote(here, here, part_send.at[which, offset], part_recv.at[which, offset], origin)
 
-    def sharing(offset, other):
-        here = landed.at[:, lax.rem(me + n - offset, n), mate]
+    def sharing(which, offset, other):
+        here = landed[which].at[lax.rem(me + n - offset, n), mate]
         dest = lax.rem(mate + other, parts)
-        return remote(here, here, mate_send.at[offset, other], mate_recv.at[offset, other], dest, "tp")
-
-    def shared(offset, other):
+        return remote(here, here, mate_send.at[which, offset, other], mate_recv.at[which, offset, other], dest, "tp")
+
+    def shared(which, offset, other):
         source = lax.rem(mate + parts - other, parts)
-        here = landed.at[:, lax.rem(me + n - offset, n), source]
-        return remote(here, here, mate_send.at[offset, other], mate_recv.at[offset, other], source, "tp")
+        here = landed[which].at[lax.rem(me + n - offset, n), source]
+        return remote(here, here, mate_send.at[which, offset, other], mate_recv.at[which, offset, other], source, "tp")
 
     own_parts = [
-        pltpu.make_async_copy(part(which, me), landed.at[which, me, mate], part_own.at[which])
+        pltpu.make_async_copy(part(which, me), landed[which].at[me, mate], part_own.at[which])
         for which in range(2)
     ]
     steps = n // 2 - 1
-    share = -(-(n - 1) // max(steps, 1))
 
     def begin():
         for copy in own_parts:
@@ -211,17 +211,18 @@
         for copy in own_parts:
             copy.wait()
         for other in range(1, parts):
-            sharing(0, other).start()
+            for which in range(2):
+                sharing(which, 0, other).start()
 
     def pass_on(offsets):
         for offset in offsets:
             for which in range(2):
                 arriving(which, offset).wait_recv()
-            for other in range(1, parts):
-                sharing(offset, other).start()
+                for other in range(1, parts):
+                    sharing(which, offset, other).start()
 
     def between(step):
-        pass_on(range(1 + (step - 1) * share, min(1 + step * share, n)))
+        pass_on(range(1 + (step - 1) * (n - 1) // steps, 1 + step * (n - 1) // steps))
 
     finish = chain_gather(n, weights, out, *gather_sems, begin=begin, between=between)
     if steps == 0:
@@ -232,8 +233,9 @@
             sending(which, offset).wait_send()
     for offset in range(n):
         for other in range(1, parts):
-            sharing(offset, other).wait_send()
-            shared(offset, other).wait_recv()
+            for which in range(2):
+                sharing(which, offset, other).wait_send()
+                shared(which, offset, other).wait_recv()
 
 
 def second_kernel(n, own, out, *sems):
@@ -245,21 +247,22 @@
     rows = tokens.shape[0] // tp_count
     cols = tokens.shape[1] // n
     anywhere = pl.BlockSpec(memory_space=pl.ANY)
-    gathered, landed = pl.pallas_call(
+    gathered, *landed = pl.pallas_call(
         functools.partial(first_kernel, n, tp_count),
         out_shape=(
             jax.ShapeDtypeStruct((n,) + weights.shape, weights.dtype),
-            jax.ShapeDtypeStruct((2, n, tp_count, rows, cols), tokens.dtype),
+            jax.ShapeDtypeStruct((n, tp_count, rows, cols), tokens.dtype),
+            jax.ShapeDtypeStruct((n, tp_count, rows, cols), tokens.dtype),
         ),
         in_specs=[anywhere] * 3,
-        out_specs=(anywhere, anywhere),
+        out_specs=(anywhere,) * 3,
         scratch_shapes=gather_semaphores(n)
         + [
             pltpu.SemaphoreType.DMA((2, n)),
             pltpu.SemaphoreType.DMA((2, n)),
             pltpu.SemaphoreType.DMA((2,)),
-            pltpu.SemaphoreType.DMA((n, tp_count)),
-            pltpu.SemaphoreType.DMA((n, tp_count)),
+            pltpu.SemaphoreType.DMA((2, n, tp_count)),
+            pltpu.SemaphoreType.DMA((2, n, tp_count)),
         ],
         compiler_params=pltpu.CompilerParams(collective_id=0, has_side_effects=True),
         cost_estimate=pl.CostEstimate(flops=0, bytes_accessed=300_000_000, transcendentals=0),
@@ -298,7 +301,9 @@
     joint_cols = head_cols + 2 * kv_cols
     joint_rows = weight_rows[:, :joint_cols]
     output_cols = weight_rows[:, joint_cols:]
-    inputs_by_cols = landed.reshape(2, blk_count * sequence_length, landed.shape[4])
+    tokens_cols, out_grad_cols = [
+        one.reshape(blk_count * sequence_length, one.shape[3]) for one in landed
+    ]
     joint_full = jnp.dot(tokens, joint_rows, preferred_element_type=jnp.float32)
     query_full = joint_full[:, :head_cols]
     key_full = joint_full[:, head_cols : head_cols + kv_cols]
@@ -363,7 +368,6 @@
         jnp.bfloat16
     )
     grads_all = gather_grads(jnp.concatenate([joined_grads, head_mix], axis=1), blk_count)
-    tokens_cols, out_grad_cols = inputs_by_cols[0], inputs_by_cols[1]
     joint_grad = leading_product(tokens_cols, grads_all[:, :joint_cols])
     query_grad = joint_grad[:, :head_cols]
     key_grad = joint_grad[:, head_cols : head_cols + kv_cols]

time: 321 us -> 319 us (level)
  local copies, waits for them, and re-layouts: 13.1 us -> 4.17 us
  waiting for transfers between devices: 0.04 us -> 7.83 us
    reduce_scatter x1, waiting for transfers between devices: 0.01 us -> 7.8 us  [on_device(): lax.psum_scatter(out_term, 'tp', scatter_dimension=1, tiled=True)]
    dot_general x2, matrix products: 5.43 us -> 9.67 us  [leading_product(): lax.dot_general(first_operand, second_operand, (((0,), (0,)), ((), ())),...]
    unnamed x19 -> x11, local copies, waits for them, and re-layouts: 5.54 us -> 1.83 us
    slice x1 -> x0, local copies, waits for them, and re-layouts: 3.46 us -> none  [on_device(): tokens_cols, out_grad_cols = (inputs_by_cols[0], inputs_by_cols[1])]
  transfers between devices with their start and end apart: 2 -> 2, of which waited for: 0 -> 1; matrix products, arithmetic and copies ran while one was open for 12% -> 8% of each run, Pallas kernels for 27% -> 27%
where the time goes in v4:
time: 319 us
  Pallas kernels  242 us (76%)
  matrix products  41 us (13%)
  between operations  14.2 us (4%)
  other arithmetic  9.13 us (3%)
  waiting for transfers between devices  7.83 us (2%)
  local copies, waits for them, and re-layouts  4.17 us (1%)
    pallas_call x1, Pallas kernels, gather_inputs(): pl.pallas_call(functools.partial(first_kernel, n, tp_count), out_shape=(j...  158 us
    pallas_call x1, Pallas kernels, gather_grads(): pl.pallas_call(functools.partial(second_kernel, n), out_shape=jax.ShapeDt...  84.6 us
    dot_general x2, matrix products, transposed_product(): lax.dot_general(first_operand, second_operand, (((1,), (1,)), ((), ())),...  16.8 us
    dot_general x2, matrix products, leading_product(): lax.dot_general(first_operand, second_operand, (((0,), (0,)), ((), ())),...  9.67 us
    reduce_scatter x1, waiting for transfers between devices, on_device(): lax.psum_scatter(out_term, 'tp', scatter_dimension=1, tiled=True)  7.8 us
  transfers between devices with their start and end apart: 2, of which 1 were waited for; matrix products, arithmetic and copies ran while one was open for 8% of the time, Pallas kernels for 27%

profile of v4, /device:TPU:0, one launch (start us, length us, event | category | flops | bytes accessed | tf_op | source)
XLA Modules:
  0.0 319.0 jit_solution(4203847482817099282)
XLA Ops:
  7.2 0.0 reduce-scatter.5.cloned.1.call-start
  7.2 1.3 copy.12
  8.5 2.4 pad_maximum_fusion.weights
  10.8 157.8 %gather_inputs.1 = (bf16[8,512,1280]{2,1,0:T(8,128)(2,1)}, bf16[8,4,96,512]{3,2,1,0:T(8,128)(2,1)}, bf16[8,4,96,512]{3,2,1,0:T(8,128)(2,1)}) custom-call(bf16[512,1280]{1,0:T(8,128)(2,1)} %pad_maximum_fusion.weights, bf16[384,4096]{1,0:T(8,128)(2,1)} %tokens.1, bf16[384,4096]{1,0:T(8,128)(2,1)} %out_grad.1), custom_call_target="tpu_custom_call" | custom-call | bytes 300000000 | tf_op jit(solution)/shard_map/gather_inputs/pallas_call | solution.py:250
  168.6 0.0 copy-start.1
  168.6 5.8 %fusion.21 = bf16[384,768]{0,1:T(8,128)(2,1)S(1)} fusion(bf16[384,4096]{1,0:T(8,128)(2,1)S(1)} %copy-done, bf16[4096,1280]{1,0:T(8,128)(2,1)} %bitcast.105), kind=kOutput, calls=%fused_computation.25 | convolution fusion | flops 2416214016 | bytes 10027008 | tf_op jit(solution)/shard_map/dot_general | solution.py:307
  174.5 4.8 %fusion.24 = bf16[512,384]{1,0:T(8,128)(2,1)S(1)} fusion(bf16[384,4096]{1,0:T(8,128)(2,1)S(1)} %copy-done.1, bf16[4096,1280]{1,0:T(8,128)(2,1)} %bitcast.106), kind=kOutput, calls=%fused_computation.28 | convolution fusion | flops 1610809344 | bytes 7733248 | tf_op jit(solution)/shard_map/dot_general | solution.py:335
  179.3 0.5 fusion.54
  179.8 0.3 fusion.17
  180.1 0.6 fusion.12
  180.8 0.6 fusion.27
  181.4 0.4 convolution_convert_fusion
  181.8 0.5 fusion.41
  182.2 0.5 fusion.38
  182.7 0.2 copy.38
  182.9 8.9 %fusion = f32[384,4096]{1,0:T(8,128)} fusion(bf16[4096,1280]{1,0:T(8,128)(2,1)} %bitcast.107, bf16[384,128]{1,0:T(8,128)(2,1)S(1)} %fusion.38, bf16[384,128]{1,0:T(8,128)(2,1)S(1)} %fusion.41, bf16[384,512]{1,0:T(8,128)(2,1)S(1)} %copy.38), kind=kOutput, calls=%fused_computation | convolution fusion | flops 2417688576 | bytes 13172736 | tf_op jit(solution)/shard_map/dot_general | solution.py:15
  191.8 0.0 reduce-scatter.5.cloned.1.call-update
  191.8 0.2 reduce-scatter.3.cloned.1.call-start
  192.1 1.5 convolution_convert_fusion.1
  193.6 7.9 %fusion.8 = f32[384,4096]{1,0:T(8,128)} fusion(bf16[384,512]{0,1:T(8,128)(2,1)S(1)} %bitcast.112, bf16[4096,1280]{1,0:T(8,128)(2,1)} %bitcast.108), kind=kOutput, calls=%fused_computation.8 | convolution fusion | flops 1610612736 | bytes 10878976 | tf_op jit(solution)/shard_map/dot_general | solution.py:15
  201.4 0.0 reduce-scatter.3.cloned.1.call-update
  201.5 0.2 copy.36
  201.7 1.0 pad_maximum_fusion.1.own
  202.7 84.6 %gather_grads.1 = bf16[8,384,1280]{2,1,0:T(8,128)(2,1)} custom-call(bf16[384,1280]{1,0:T(8,128)(2,1)} %pad_maximum_fusion.1.own), custom_call_target="tpu_custom_call" | custom-call | bytes 250000000 | tf_op jit(solution)/shard_map/gather_grads/pallas_call | solution.py:276
  287.3 5.0 %fusion.4 = f32[512,768]{1,0:T(8,128)S(1)} fusion(bf16[3072,512]{1,0:T(8,128)(2,1)S(1)} %bitcast.115, bf16[3072,1280]{1,0:T(8,128)(2,1)} %bitcast.102), kind=kOutput, calls=%fused_computation.4 | convolution fusion | flops 2415919104 | bytes 9437184 | tf_op jit(solution)/shard_map/dot_general | solution.py:21
  292.4 1.1 slice.49
  293.4 0.8 fusion.53
  294.3 0.6 copy-done.3
  294.8 4.7 %fusion.10 = f32[512,512]{1,0:T(8,128)} fusion(bf16[3072,512]{1,0:T(8,128)(2,1)S(1)} %bitcast.114, bf16[3072,1280]{1,0:T(8,128)(2,1)} %bitcast.103), kind=kOutput, calls=%fused_computation.10 | convolution fusion | flops 1610612736 | bytes 7340032 | tf_op jit(solution)/shard_map/dot_general | solution.py:21
  299.5 2.4 convert_element_type.80
  301.9 7.8 %reduce-scatter.3.cloned.1.call-done = f32[384,1024]{1,0:T(8,128)} async-done(((f32[384,4096]{1,0:T(8,128)}), f32[384,1024]{1,0:T(8,128)}) %reduce-scatter.3.cloned.1.call-update) | async-done | bytes 1572880 | tf_op jit(solution)/shard_map/reduce_scatter | solution.py:331
  309.7 2.4 convert_element_type.67
  (10 shorter events, 0.1 us)
Async XLA Ops:
  7.2 292.3 %reduce-scatter.5.cloned.1.call-start = ((), (), s32[]{:S(2)}) async-start(), calls=%async_computation.3 | async-start | bytes 7864320 | tf_op jit(solution)/shard_map/reduce_scatter | solution.py:367
  10.8 157.8 %copy-start = (bf16[384,4096]{1,0:T(8,128)(2,1)S(1)}, bf16[384,4096]{1,0:T(8,128)(2,1)}, u32[]{:S(2)}) copy-start(bf16[384,4096]{1,0:T(8,128)(2,1)} %tokens.1) | copy-start | bytes 9437188
  168.6 5.8 %copy-start.1 = (bf16[384,4096]{1,0:T(8,128)(2,1)S(1)}, bf16[384,4096]{1,0:T(8,128)(2,1)}, u32[]{:S(2)}) copy-start(bf16[384,4096]{1,0:T(8,128)(2,1)} %out_grad.1) | copy-start | bytes 9437188
  174.4 6.9 %copy-start.2 = (bf16[384,768]{0,1:T(8,128)(2,1)}, bf16[384,768]{0,1:T(8,128)(2,1)S(1)}, u32[]{:S(2)}) copy-start(bf16[384,768]{0,1:T(8,128)(2,1)S(1)} %fusion.21) | copy-start | bytes 1769476
  191.8 117.9 %reduce-scatter.3.cloned.1.call-start = ((), (), s32[]{:S(2)}) async-start(), calls=%async_computation.2 | async-start | bytes 7864320 | tf_op jit(solution)/shard_map/reduce_scatter | solution.py:331
  202.7 84.6 %copy-start.4 = (bf16[8,4,96,512]{3,2,1,0:T(8,128)(2,1)S(1)}, bf16[8,4,96,512]{3,2,1,0:T(8,128)(2,1)}, u32[]{:S(2)}) copy-start(bf16[8,4,96,512]{3,2,1,0:T(8,128)(2,1)} %get-tuple-element.41) | copy-start | bytes 9437188
  292.3 2.5 copy-start.3
Sparse Core Ops, SparseCore 0:
  192.0 56.6 reduce-scatter.4
  251.3 58.3 reduce-scatter.2
